TPU v7x, 32 devices: a whole 2x2x4 slice. The times are simulated.
32 devices in a mesh: groups: 2 (over y), tensor: 4 (over z), expert: 4 (over x, core).
Axes of the slice: x: 2, y: 2, z: 4, core: 2. Of those that a mesh axis runs over, the one named last changes fastest.
Arguments:
- tokens: bfloat16 [1024, 3072], P(('groups', 'expert'), 'tensor'), parts along dimension 0, may hold values from -6 to 6
- expert_ids: int32 [1024, 2], P(('groups', 'expert')), parts along dimension 0, may hold values from 0 to 7, all different within a row; in each aligned block of 128 rows (0 to 127, 128 to 255, ...) at most 64 rows name the same one
- router_logits: float32 [1024, 2], P(('groups', 'expert')), parts along dimension 0, may hold values from -6 to 6
- gate_weight: bfloat16 [8, 3072, 8192], P('expert', None, 'tensor'), may hold values from -0.109375 to 0.109375
- up_weight: bfloat16 [8, 3072, 8192], P('expert', None, 'tensor'), may hold values from -0.109375 to 0.109375
- down_weight: bfloat16 [8, 8192, 3072], P('expert', 'tensor'), may hold values from -0.0625 to 0.0625
Outputs:
- mixed: bfloat16 [1024, 3072], P(('groups', 'expert'), 'tensor'), parts along dimension 0
There are 2 independent parts, one for each index of `groups`. A program takes and returns all parts, laid end to end along the dimension named above; an argument that names none is the same for every part. Nothing has to cross between parts.
Inputs may be any that keep to these rules, and one draw needn't show every extreme that they name: `expert_ids`: each row names two different experts. In each aligned block of 128 rows (the rows of one index of expert) no expert is named more than 64 times, a bound that some block reaches.
All inputs are finite; a program needn't handle non-finite values.
Results may differ from a plain program's by a relative error of at most 0.01.
Values may be sent and summed in bfloat16 or wider, within the bound.
A program may use at most 192 MiB of HBM per device.

v0:
```python
import jax
import jax.numpy as jnp
from jax import lax
from jax.sharding import PartitionSpec as P


def route(ids, experts, cap):
    flat = ids.reshape(-1)
    onehot = (flat[:, None] == jnp.arange(experts, dtype=jnp.int32)[None, :]).astype(jnp.int32)
    before = jnp.cumsum(onehot, axis=0) - onehot
    slot = jnp.sum(before * onehot, axis=1)
    return (flat * cap + slot).reshape(ids.shape)


def placement_table(dest, slots_all):
    slot_ids = jnp.arange(slots_all, dtype=jnp.int32)[:, None]
    table = (slot_ids == dest[None, :, 0]).astype(jnp.float32) + (
        slot_ids == dest[None, :, 1]
    ).astype(jnp.float32)
    return table.astype(jnp.bfloat16)


def on_device(tokens, expert_ids, router_logits, gate_weight, up_weight, down_weight):
    tok_rows = tokens.shape[0]
    local_experts = gate_weight.shape[0]
    experts = local_experts * lax.axis_size("expert")
    cap = tok_rows // 2
    dest = route(expert_ids, experts, cap)
    table = placement_table(dest, experts * cap)
    whole = lax.all_gather(tokens, "tensor", axis=1, tiled=True)
    buffer = jnp.dot(table, whole, preferred_element_type=jnp.float32).astype(jnp.bfloat16)
    buffer = buffer.reshape(experts, 1, cap, whole.shape[1])
    arrived = lax.all_to_all(buffer, "expert", split_axis=0, concat_axis=1, tiled=True)
    rows = arrived.reshape(local_experts, -1, whole.shape[1])
    gate = jnp.einsum("erd,edf->erf", rows, gate_weight, preferred_element_type=jnp.float32)
    up = jnp.einsum("erd,edf->erf", rows, up_weight, preferred_element_type=jnp.float32)
    hidden = (jax.nn.silu(gate) * up).astype(jnp.bfloat16)
    terms = jnp.einsum("erf,efd->erd", hidden, down_weight, preferred_element_type=jnp.float32)
    share = lax.psum_scatter(terms.astype(jnp.bfloat16), "tensor", scatter_dimension=2, tiled=True)
    width_dev = share.shape[2]
    share = share.reshape(local_experts, -1, cap, width_dev)
    back = lax.all_to_all(share, "expert", split_axis=1, concat_axis=0, tiled=True)
    flat = back.reshape(experts * cap, width_dev)
    probs = jax.nn.softmax(router_logits, axis=-1)
    picked = jnp.take(flat, dest, axis=0)
    mixed = jnp.sum(picked.astype(jnp.float32) * probs[..., None], axis=1)
    return mixed.astype(jnp.bfloat16)


def solution(mesh):
    placed = (
        P(("groups", "expert"), "tensor"),
        P(("groups", "expert"), None),
        P(("groups", "expert"), None),
        P("expert", None, "tensor"),
        P("expert", None, "tensor"),
        P("expert", "tensor", None),
    )
    return jax.shard_map(
        on_device,
        mesh=mesh,
        in_specs=placed,
        out_specs=P(("groups", "expert"), "tensor"),
        check_vma=False,
    )
```

profile of v0, /device:TPU:0, one launch (start us, length us, event | category | flops | bytes accessed | tf_op | source)
XLA Modules:
  0.0 194.4 jit_solution(13844574419652546398)
XLA Ops:
  6.5 0.8 copy.33
  7.3 0.1 eq.59
  7.5 0.1 eq.55
  7.6 0.6 reduce-window.6
  8.2 0.2 slice_reduce_fusion
  8.6 0.1 reduce_sum.30
  8.8 0.7 compare_and_fusion
  9.5 21.5 %all_gather.3 = bf16[128,3072]{1,0:T(8,128)(2,1)S(1)} all-gather(bf16[128,768]{1,0:T(8,128)(2,1)} %param.6), channel_id=1, replica_groups=mesh['groups'=2,'tensor'=4,'expert'=4] {'tensor'}, dimensions={1}, use_global_device_ids=true | all-gather | bytes 983040 | tf_op jit(solution)/shard_map/all_gather | solution.py:30
  31.0 1.0 convolution_convert_fusion.1
  32.0 39.5 %all_to_all.30 = bf16[8,1,64,3072]{3,2,1,0:T(8,128)(2,1)S(1)} all-to-all(bf16[8,1,64,3072]{3,2,1,0:T(8,128)(2,1)S(1)} %bitcast.33), channel_id=1, replica_groups=mesh['groups'=2,'tensor'=4,'expert'=4] {'expert'}, dimensions={0} | all-to-all | bytes 6291456 | tf_op jit(solution)/shard_map/all_to_all | solution.py:33
  71.5 0.2 copy.38
  71.7 11.6 %fusion.7 = f32[2,256,2048]{2,1,0:T(8,128)S(1)} fusion(bf16[2,256,3072]{2,1,0:T(8,128)(2,1)S(1)} %bitcast.35, bf16[2,3072,2048]{2,1,0:T(8,128)(2,1)} %param.9), kind=kOutput, calls=%fused_computation.27 | convolution fusion | flops 6442450944 | bytes 32505856 | tf_op jit(solution)/shard_map/erd,edf->erf/dot_general | solution.py:35
  83.3 12.2 %multiply_convert_fusion = bf16[2,256,2048]{2,1,0:T(8,128)(2,1)S(1)} fusion(f32[2,256,2048]{2,1,0:T(8,128)S(1)} %fusion.7, bf16[2,256,3072]{2,1,0:T(8,128)(2,1)S(1)} %bitcast.36, bf16[2,3072,2048]{2,1,0:T(8,128)(2,1)} %param.10), kind=kOutput, calls=%fused_computation.3 | convolution fusion | flops 6448742400 | bytes 34603008 | tf_op jit(solution)/shard_map/erd,edf->erf/dot_general | solution.py:36
  95.5 12.8 %convolution_convert_fusion = bf16[2,256,3072]{2,1,0:T(8,128)(2,1)} fusion(bf16[2,256,2048]{2,1,0:T(8,128)(2,1)S(1)} %multiply_convert_fusion, bf16[2,2048,3072]{2,1,0:T(8,128)(2,1)} %param.11), kind=kOutput, calls=%fused_computation.1 | convolution fusion | flops 6444023808 | bytes 30408704 | tf_op jit(solution)/shard_map/erf,efd->erd/dot_general | solution.py:38
  108.3 58.8 %reduce-scatter.2.cloned.1.call-done = bf16[2,256,768]{2,1,0:T(8,128)(2,1)} async-done(((bf16[2,256,3072]{2,1,0:T(8,128)(2,1)}), bf16[2,256,768]{2,1,0:T(8,128)(2,1)}) %reduce-scatter.2.cloned.1.call-update) | async-done | bytes 786448 | tf_op jit(solution)/shard_map/reduce_scatter | solution.py:39
  167.1 2.1 %copy.39 = bf16[2,4,64,768]{3,2,0,1:T(8,128)(2,1)} copy(bf16[2,4,64,768]{3,2,1,0:T(8,128)(2,1)} %bitcast.37) | data formatting | bytes 1572864 | tf_op jit(solution)/shard_map/reshape | solution.py:41
  169.2 3.7 %all-to-all-start.1 = ((bf16[2,4,64,768]{3,2,0,1:T(8,128)(2,1)}), bf16[2,4,64,768]{3,2,0,1:T(8,128)(2,1)S(1)}, u32[]{:S(2)}, u32[]{:S(2)}) async-start(bf16[2,4,64,768]{3,2,0,1:T(8,128)(2,1)} %copy.39), calls=%async_computation.2 | async-start | bytes 1572864 | tf_op jit(solution)/shard_map/all_to_all | solution.py:42
  173.0 0.1 reshape.51
  173.1 0.1 copy.36
  173.3 0.1 copy.41
  173.4 10.8 %all-to-all-done.1 = bf16[2,4,64,768]{3,2,0,1:T(8,128)(2,1)S(1)} async-done(((bf16[2,4,64,768]{3,2,0,1:T(8,128)(2,1)}), bf16[2,4,64,768]{3,2,0,1:T(8,128)(2,1)S(1)}, u32[]{:S(2)}, u32[]{:S(2)}) %all-to-all-start.1) | async-done | bytes 786464 | tf_op jit(solution)/shard_map/all_to_all | solution.py:42
  184.3 1.2 gather_fusion
  185.5 0.1 reshape.50
  185.6 1.9 multiply_reduce_fusion
  (16 shorter events, 0.4 us)
Async XLA Ops:
  6.5 160.6 %reduce-scatter.2.cloned.1.call-start = ((), (), s32[]{:S(2)}) async-start(), calls=%async_computation.3 | async-start | bytes 3932160 | tf_op jit(solution)/shard_map/reduce_scatter | solution.py:39
  108.2 65.0 %copy-start = (f32[128,2]{0,1:T(2,128)S(1)}, f32[128,2]{0,1:T(2,128)}, u32[]{:S(2)}) copy-start(f32[128,2]{0,1:T(2,128)} %param.8) | copy-start | bytes 3076
  169.2 15.1 %all-to-all-start.1 = ((bf16[2,4,64,768]{3,2,0,1:T(8,128)(2,1)}), bf16[2,4,64,768]{3,2,0,1:T(8,128)(2,1)S(1)}, u32[]{:S(2)}, u32[]{:S(2)}) async-start(bf16[2,4,64,768]{3,2,0,1:T(8,128)(2,1)} %copy.39), calls=%async_computation.2 | async-start | bytes 1572864 | tf_op jit(solution)/shard_map/all_to_all | solution.py:42
Sparse Core Ops, SparseCore 0:
  108.4 58.6 reduce-scatter.1
where the time goes:
time: 195 us; the launch traced here: 194 us
  waiting for transfers between devices  69.7 us (36%)
  blocking collectives  61 us (31%)
  matrix products  37.5 us (19%)
  between operations  13.5 us (7%)
  local copies, waits for them, and re-layouts  5.59 us (3%)
  starting transfers between devices  3.68 us (2%)
  other arithmetic  3.42 us (2%)
    reduce_scatter x1, waiting for transfers between devices, on_device(): lax.psum_scatter(terms.astype(jnp.bfloat16), 'tensor', scatter_dimension=...  58.8 us
    all_to_all x1, blocking collectives, on_device(): lax.all_to_all(buffer, 'expert', split_axis=0, concat_axis=1, tiled=True)  39.5 us
    all_gather x1, blocking collectives, on_device(): whole = lax.all_gather(tokens, 'tensor', axis=1, tiled=True)  21.5 us
    dot_general x1, matrix products, on_device(): jnp.einsum('erf,efd->erd', hidden, down_weight, preferred_element_type=jn...  12.8 us
    dot_general x1, matrix products, on_device(): jnp.einsum('erd,edf->erf', rows, up_weight, preferred_element_type=jnp.fl...  12.2 us
    dot_general x1, matrix products, on_device(): jnp.einsum('erd,edf->erf', rows, gate_weight, preferred_element_type=jnp....  11.6 us
    all_to_all x1, waiting for transfers between devices, on_device(): lax.all_to_all(share, 'expert', split_axis=1, concat_axis=0, tiled=True)  10.8 us
  transfers between devices with their start and end apart: 2, of which 2 were waited for; matrix products, arithmetic and copies ran while one was open for 0% of the time, Pallas kernels for 0%

commit v1 on v0

--- a/solution.py
+++ b/solution.py
@@ -1,7 +1,317 @@
+import functools
+
 import jax
 import jax.numpy as jnp
 from jax import lax
+from jax.experimental import pallas as pl
+from jax.experimental.pallas import tpu as pltpu
 from jax.sharding import PartitionSpec as P
+
+MESH = pl.DeviceIdType.MESH
+F32 = jnp.float32
+BF16 = jnp.bfloat16
+PAIRS = 4
+CHUNKS = 2
+
+
+def remote(src, dst, send_sem, recv_sem, device):
+    return pltpu.make_async_remote_copy(
+        src_ref=src,
+        dst_ref=dst,
+        send_sem=send_sem,
+        recv_sem=recv_sem,
+        device_id=device,
+        device_id_type=MESH,
+    )
+
+
+def layer_kernel(
+    meta_ref, tok_ref, gate_hbm, up_hbm, down_hbm, out_ref,
+    metas, xg, place, blend, rows, acc, hidden, wgu, wdn, ybuf,
+    give, keep, core_in, x_out, x_in, z_out, z_in,
+    ms, mr, zs, zr, xs, xr, ss, sr, gsem, dsem, cs, cr, xs2, xr2, zs2, zr2,
+):
+    e = lax.axis_index("expert")
+    z = lax.axis_index("tensor")
+    x = e // 2
+    c = e % 2
+    sib = x * 2 + 1 - c
+    opp = (1 - x) * 2 + c
+    diag = (1 - x) * 2 + 1 - c
+    zi = [z, z + 1 - 2 * (z % 2), (z + 2) % 4, 3 - z]
+    tok_rows, width = tok_ref.shape
+    half = tok_rows // 2
+    ff = wgu.shape[3]
+    nt = 256
+
+    def gu_copies(s):
+        i, j = s // 2, s % 2
+        src = pl.ds(pl.multiple_of(zi[i] * width, width), width)
+        slot = s % PAIRS
+        return [
+            pltpu.make_async_copy(gate_hbm.at[j, src, :], wgu.at[slot, 0], gsem.at[slot, 0]),
+            pltpu.make_async_copy(up_hbm.at[j, src, :], wgu.at[slot, 1], gsem.at[slot, 1]),
+        ]
+
+    order = [2, 3, 1, 0]
+
+    def down_copies(k):
+        src = pl.ds(pl.multiple_of(zi[order[k]] * width, width), width)
+        slot = k % CHUNKS
+        return [
+            pltpu.make_async_copy(down_hbm.at[j, :, src], wdn.at[slot, j], dsem.at[slot, j])
+            for j in range(2)
+        ]
+
+    for s in range(PAIRS):
+        for cp in gu_copies(s):
+            cp.start()
+
+    barrier = pltpu.get_barrier_semaphore()
+    for peer in (sib, opp, diag):
+        pl.semaphore_signal(barrier, inc=1, device_id={"expert": peer}, device_id_type=MESH)
+    for i in (1, 2, 3):
+        pl.semaphore_signal(barrier, inc=1, device_id={"tensor": zi[i]}, device_id_type=MESH)
+    pl.semaphore_wait(barrier, 6)
+
+    pending = []
+    for n, peer in enumerate((sib, opp, diag)):
+        cp = remote(meta_ref, metas.at[e], ms.at[n], mr.at[n], {"expert": peer})
+        cp.start()
+        pending.append(cp)
+
+    def send_x(i, src):
+        cp = remote(src, xg.at[zi[i], e], xs.at[i], xr.at[i], {"expert": opp})
+        cp.start()
+        pending.append(cp)
+
+    def send_sib(kind, i, src, owner):
+        cp = remote(src, xg.at[zi[i], owner], ss.at[kind, i], sr.at[kind, i], {"expert": sib})
+        cp.start()
+        pending.append(cp)
+
+    send_x(0, tok_ref)
+    for i in (1, 2, 3):
+        cp = remote(tok_ref, xg.at[z, e], zs.at[i - 1], zr.at[i - 1], {"tensor": zi[i]})
+        cp.start()
+        pending.append(cp)
+    send_sib(0, 0, tok_ref, e)
+
+    for k in range(CHUNKS):
+        for cp in down_copies(k):
+            cp.start()
+
+    xg[z, e] = tok_ref[...]
+    metas[e] = meta_ref[...]
+
+    def arrived_z(i):
+        here = xg.at[zi[i], e]
+        remote(here, here, zs.at[i - 1], zr.at[i - 1], {"tensor": zi[i]}).wait_recv()
+        send_x(i, here)
+        send_sib(0, i, here, e)
+
+    def arrived_x(i):
+        here = xg.at[zi[i], opp]
+        remote(here, here, xs.at[i], xr.at[i], {"expert": opp}).wait_recv()
+        send_sib(1, i, here, opp)
+
+    def arrived_sib(i):
+        for kind, owner in ((0, sib), (1, diag)):
+            here = xg.at[zi[i], owner]
+            remote(here, here, ss.at[kind, i], sr.at[kind, i], {"expert": sib}).wait_recv()
+
+    for n, peer in enumerate((sib, opp, diag)):
+        here = metas.at[peer]
+        remote(here, here, ms.at[n], mr.at[n], {"expert": peer}).wait_recv()
+
+    lane = lax.broadcasted_iota(jnp.int32, (tok_rows, tok_rows), 1)
+    row = lax.broadcasted_iota(jnp.int32, (tok_rows, tok_rows), 0)
+    earlier = (lane < row).astype(F32).astype(BF16)
+    lane_f = lane.astype(F32)
+    names = (lane + 2 * e).astype(F32)
+    left = lane < half
+    for b in range(4):
+        cols = metas[b].T
+        id0, id1 = cols[:, 0:1], cols[:, 1:2]
+        l0, l1 = cols[:, 2:3], cols[:, 3:4]
+        top = jnp.maximum(l0, l1)
+        e0, e1 = jnp.exp(l0 - top), jnp.exp(l1 - top)
+        total = e0 + e1
+        hit0 = (id0 == names).astype(F32)
+        hit1 = (id1 == names).astype(F32)
+        named = hit0 + hit1
+        prob = hit0 * (e0 / total) + hit1 * (e1 / total)
+        before = jnp.dot(earlier, named.astype(BF16), preferred_element_type=F32)
+        slot = jnp.where(left, before[:, 0:1], before[:, 1:2] + half)
+        used = jnp.where(left, named[:, 0:1], named[:, 1:2])
+        amount = jnp.where(left, prob[:, 0:1], prob[:, 1:2])
+        same = (slot == lane_f).astype(F32)
+        place[b] = (same * used).T.astype(BF16)
+        blend[b] = (same * amount).astype(BF16)
+
+    def fill(i):
+        for b in range(4):
+            got = jnp.dot(place[b], xg[zi[i], b], preferred_element_type=F32).astype(BF16)
+            for j in range(2):
+                rows[j, pl.ds(b * half, half), :] = got[j * half:(j + 1) * half]
+
+    def gate_up(i, j):
+        s = i * 2 + j
+        slot = s % PAIRS
+        for cp in gu_copies(s):
+            cp.wait()
+
+        def tile(n, carry):
+            cols = pl.ds(pl.multiple_of(n * nt, nt), nt)
+            g = jnp.dot(rows[j], wgu[slot, 0, :, cols], preferred_element_type=F32)
+            u = jnp.dot(rows[j], wgu[slot, 1, :, cols], preferred_element_type=F32)
+            if i > 0:
+                g = g + acc[j, 0, :, cols]
+                u = u + acc[j, 1, :, cols]
+            if i < 3:
+                acc[j, 0, :, cols] = g
+                acc[j, 1, :, cols] = u
+            else:
+                hidden[j, :, cols] = (g / (1.0 + jnp.exp(-g)) * u).astype(BF16)
+            return carry
+
+        lax.fori_loop(0, ff // nt, tile, 0)
+        if s + PAIRS < 8:
+            for cp in gu_copies(s + PAIRS):
+                cp.start()
+
+    arrived_x(0)
+    arrived_z(1)
+    arrived_sib(0)
+    fill(0)
+    gate_up(0, 0)
+    arrived_z(2)
+    gate_up(0, 1)
+    arrived_x(1)
+    arrived_z(3)
+    arrived_sib(1)
+    fill(1)
+    gate_up(1, 0)
+    arrived_x(2)
+    gate_up(1, 1)
+    arrived_sib(2)
+    fill(2)
+    gate_up(2, 0)
+    arrived_x(3)
+    gate_up(2, 1)
+    arrived_sib(3)
+    fill(3)
+    gate_up(3, 0)
+    gate_up(3, 1)
+
+    def down(k):
+        slot = k % CHUNKS
+        for cp in down_copies(k):
+            cp.wait()
+
+        def tile(n, carry):
+            cols = pl.ds(pl.multiple_of(n * nt, nt), nt)
+            for j in range(2):
+                y = jnp.dot(hidden[j], wdn[slot, j, :, cols], preferred_element_type=F32).astype(BF16)
+                for b in range(4):
+                    ybuf[b, pl.ds(j * half, half), cols] = y[b * half:(b + 1) * half]
+            return carry
+
+        lax.fori_loop(0, width // nt, tile, 0)
+        if k + CHUNKS < 4:
+            for cp in down_copies(k + CHUNKS):
+                cp.start()
+        for at in range(2):
+            b = at * 2 + 1 - c
+            give[k, at] = jnp.dot(blend[b], ybuf[b], preferred_element_type=F32).astype(BF16)
+        cp = remote(give.at[k], core_in.at[k], cs.at[k], cr.at[k], {"expert": sib})
+        cp.start()
+        pending.append(cp)
+        for at in range(2):
+            b = at * 2 + c
+            keep[k, at] = jnp.dot(blend[b], ybuf[b], preferred_element_type=F32).astype(BF16)
+
+    def over_x(k):
+        here = core_in.at[k]
+        remote(here, here, cs.at[k], cr.at[k], {"expert": sib}).wait_recv()
+        x_out[k] = (keep[k, 1 - x].astype(F32) + core_in[k, 1 - x].astype(F32)).astype(BF16)
+        cp = remote(x_out.at[k], x_in.at[k], xs2.at[k], xr2.at[k], {"expert": opp})
+        cp.start()
+        pending.append(cp)
+
+    def summed(k):
+        here = x_in.at[k]
+        remote(here, here, xs2.at[k], xr2.at[k], {"expert": opp}).wait_recv()
+        return keep[k, x].astype(F32) + core_in[k, x].astype(F32) + x_in[k].astype(F32)
+
+    def over_z(k):
+        i = order[k]
+        z_out[k] = summed(k).astype(BF16)
+        cp = remote(z_out.at[k], z_in.at[k], zs2.at[k], zr2.at[k], {"tensor": zi[i]})
+        cp.start()
+        pending.append(cp)
+
+    for k in range(4):
+        down(k)
+        over_x(k)
+        if k:
+            over_z(k - 1)
+    mine = summed(3)
+    for k in range(3):
+        here = z_in.at[k]
+        remote(here, here, zs2.at[k], zr2.at[k], {"tensor": zi[order[k]]}).wait_recv()
+        mine = mine + z_in[k].astype(F32)
+    out_ref[...] = mine.astype(BF16)
+    for cp in pending:
+        cp.wait_send()
+
+
+def fused(tokens, expert_ids, router_logits, gate_weight, up_weight, down_weight):
+    tok_rows, width = tokens.shape
+    ff = gate_weight.shape[2]
+    half = tok_rows // 2
+    slots = 4 * half
+    meta = jnp.concatenate(
+        [expert_ids.T.astype(F32), router_logits.T, jnp.zeros((4, tok_rows), F32)], axis=0
+    )
+    vmem = pl.BlockSpec(memory_space=pltpu.VMEM)
+    anywhere = pl.BlockSpec(memory_space=pl.ANY)
+    dma = pltpu.SemaphoreType.DMA
+    flops = 2 * 2 * slots * 3 * (4 * width) * ff
+    return pl.pallas_call(
+        layer_kernel,
+        out_shape=jax.ShapeDtypeStruct((tok_rows, width), BF16),
+        in_specs=[vmem, vmem, anywhere, anywhere, anywhere],
+        out_specs=vmem,
+        scratch_shapes=[
+            pltpu.VMEM((4, 8, tok_rows), F32),
+            pltpu.VMEM((4, 4, tok_rows, width), BF16),
+            pltpu.VMEM((4, tok_rows, tok_rows), BF16),
+            pltpu.VMEM((4, tok_rows, tok_rows), BF16),
+            pltpu.VMEM((2, slots, width), BF16),
+            pltpu.VMEM((2, 2, slots, ff), F32),
+            pltpu.VMEM((2, slots, ff), BF16),
+            pltpu.VMEM((PAIRS, 2, width, ff), BF16),
+            pltpu.VMEM((CHUNKS, 2, ff, width), BF16),
+            pltpu.VMEM((4, tok_rows, width), BF16),
+            pltpu.VMEM((4, 2, tok_rows, width), BF16),
+            pltpu.VMEM((4, 2, tok_rows, width), BF16),
+            pltpu.VMEM((4, 2, tok_rows, width), BF16),
+            pltpu.VMEM((4, tok_rows, width), BF16),
+            pltpu.VMEM((4, tok_rows, width), BF16),
+            pltpu.VMEM((3, tok_rows, width), BF16),
+            pltpu.VMEM((3, tok_rows, width), BF16),
+            dma((3,)), dma((3,)), dma((3,)), dma((3,)), dma((4,)), dma((4,)),
+            dma((2, 4)), dma((2, 4)), dma((PAIRS, 2)), dma((CHUNKS, 2)),
+            dma((4,)), dma((4,)), dma((4,)), dma((4,)), dma((3,)), dma((3,)),
+        ],
+        compiler_params=pltpu.CompilerParams(
+            collective_id=0, has_side_effects=True, vmem_limit_bytes=64 * 1024 * 1024
+        ),
+        cost_estimate=pl.CostEstimate(
+            flops=flops, bytes_accessed=12 * 4 * width * ff, transcendentals=2 * slots * ff
+        ),
+    )(meta, tokens, gate_weight, up_weight, down_weight)
 
 
 def route(ids, experts, cap):
@@ -56,8 +366,16 @@
         P("expert", None, "tensor"),
         P("expert", "tensor", None),
     )
+    sizes = (mesh.shape["expert"], mesh.shape["tensor"])
+
+    def per_device(*args):
+        tokens, gate_weight = args[0], args[3]
+        fits = sizes == (4, 4) and gate_weight.shape[0] == 2 and tokens.shape[1] % 256 == 0
+        fits = fits and tokens.shape[0] == 128 and gate_weight.shape[2] % 256 == 0
+        return (fused if fits else on_device)(*args)
+
     return jax.shard_map(
-        on_device,
+        per_device,
         mesh=mesh,
         in_specs=placed,
         out_specs=P(("groups", "expert"), "tensor"),

time: 195 us -> 78.6 us (0.40)
  Pallas kernels: 0 us -> 74.7 us
  waiting for transfers between devices: 69.7 us -> 0 us
  blocking collectives: 61 us -> 0 us
  matrix products: 37.5 us -> 0 us
  between operations: 13.5 us -> 0.01 us
  local copies, waits for them, and re-layouts: 5.59 us -> 1.7 us
  starting transfers between devices: 3.68 us -> 0 us
    pallas_call x0 -> x1, Pallas kernels: none -> 74.7 us  [fused(): pl.pallas_call(layer_kernel, out_shape=jax.ShapeDtypeStruct((tok_rows, wi...]
    reduce_scatter x1 -> x0, waiting for transfers between devices: 58.8 us -> none  [on_device(): lax.psum_scatter(terms.astype(jnp.bfloat16), 'tensor', scatter_dimension=...]
    all_to_all x1 -> x0, blocking collectives: 39.5 us -> none  [on_device(): lax.all_to_all(buffer, 'expert', split_axis=0, concat_axis=1, tiled=True)]
    dot_general x4 -> x0, matrix products: 37.5 us -> none  [the longest x1 12.8 us: on_device(): jnp.einsum('erf,efd->erd', hidden, down_weight, preferred_element_type=jn...]
    all_gather x1 -> x0, blocking collectives: 21.5 us -> none  [on_device(): whole = lax.all_gather(tokens, 'tensor', axis=1, tiled=True)]
    all_to_all x1 -> x0, waiting for transfers between devices: 10.8 us -> none  [on_device(): lax.all_to_all(share, 'expert', split_axis=1, concat_axis=0, tiled=True)]
    all_to_all x1 -> x0, starting transfers between devices: 3.67 us -> none  [on_device(): lax.all_to_all(share, 'expert', split_axis=1, concat_axis=0, tiled=True)]
    reshape x1 -> x0, local copies, waits for them, and re-layouts: 2.06 us -> none  [on_device(): share = share.reshape(local_experts, -1, cap, width_dev)]
  transfers between devices with their start and end apart: 2 -> 0, of which waited for: 2 -> 0; matrix products, arithmetic and copies ran while one was open for 0% -> 0% of each run, Pallas kernels for 0% -> 0%
where the time goes in v1:
time: 78.6 us; the launch traced here: 78.4 us
  Pallas kernels  74.7 us (95%)
  other arithmetic  2.02 us (3%)
  local copies, waits for them, and re-layouts  1.7 us (2%)
    pallas_call x1, Pallas kernels, fused(): pl.pallas_call(layer_kernel, out_shape=jax.ShapeDtypeStruct((tok_rows, wi...  74.7 us
    unnamed x1, local copies, waits for them, and re-layouts  1.62 us

profile of v1, /device:TPU:0, one launch (start us, length us, event | category | flops | bytes accessed | tf_op | source)
XLA Modules:
  0.0 78.4 jit_solution(1767005611504460180)
XLA Ops:
  0.0 0.1 pad.2.clone
  0.1 0.7 convert_bitcast_fusion
  0.8 1.3 %maximum_maximum_fusion.meta_ref = f32[8,128]{1,0:T(8,128)} fusion(f32[2,128]{1,0:T(2,128)} %bitcast.3, f32[2,128]{1,0:T(2,128)S(1)} %convert_bitcast_fusion, f32[8]{0:T(128)S(1)} %pad.2.clone), kind=kLoop, calls=%fused_computation | loop fusion | flops 2048 | bytes 6176 | tf_op jit(solution)/shard_map/concatenate | solution.py:274
  2.1 74.7 %shard_map.64 = bf16[128,768]{1,0:T(8,128)(2,1)} custom-call(f32[8,128]{1,0:T(8,128)} %maximum_maximum_fusion.meta_ref, bf16[128,768]{1,0:T(8,128)(2,1)} %tok_ref.1, bf16[2,3072,2048]{2,1,0:T(8,128)(2,1)} %gate_hbm.1, bf16[2,3072,2048]{2,1,0:T(8,128)(2,1)} %up_hbm.1, bf16[2,2048,3072]{2,1,0:T(8,128)(2,1)} %down_hbm.1), custom_call_target="tpu_custom_call" | custom-call | flops 19327352832 | bytes 75497472 | tf_op jit(solution)/shard_map/pallas_call | solution.py:281
  76.8 1.6 %copy.8 = bf16[128,768]{1,0:T(8,128)(2,1)} copy(bf16[128,768]{1,0:T(8,128)(2,1)} %shard_map.64) | data formatting | bytes 393216
  (1 shorter events, 0.0 us)

commit v2 on v1

--- a/solution.py
+++ b/solution.py
@@ -38,11 +38,14 @@
     sib = x * 2 + 1 - c
     opp = (1 - x) * 2 + c
     diag = (1 - x) * 2 + 1 - c
-    zi = [z, z + 1 - 2 * (z % 2), (z + 2) % 4, 3 - z]
+    mate, other = z + 1 - 2 * (z % 2), 3 - z
+    zi = [z, mate, 2 - z // 2, 3 * (1 - z // 2)]
+    inner = (z + 1) // 2 == 1
+    end = (z + 1) // 2 != 1
     tok_rows, width = tok_ref.shape
     half = tok_rows // 2
     ff = wgu.shape[3]
-    nt = 256
+    nt = ff // 2
 
     def gu_copies(s):
         i, j = s // 2, s % 2
@@ -53,7 +56,7 @@
             pltpu.make_async_copy(up_hbm.at[j, src, :], wgu.at[slot, 1], gsem.at[slot, 1]),
         ]
 
-    order = [2, 3, 1, 0]
+    order = [3, 2, 1, 0]
 
     def down_copies(k):
         src = pl.ds(pl.multiple_of(zi[order[k]] * width, width), width)
@@ -70,9 +73,17 @@
     barrier = pltpu.get_barrier_semaphore()
     for peer in (sib, opp, diag):
         pl.semaphore_signal(barrier, inc=1, device_id={"expert": peer}, device_id_type=MESH)
-    for i in (1, 2, 3):
-        pl.semaphore_signal(barrier, inc=1, device_id={"tensor": zi[i]}, device_id_type=MESH)
-    pl.semaphore_wait(barrier, 6)
+    pl.semaphore_signal(barrier, inc=1, device_id={"tensor": mate}, device_id_type=MESH)
+
+    @pl.when(inner)
+    def _():
+        pl.semaphore_signal(barrier, inc=1, device_id={"tensor": other}, device_id_type=MESH)
+        pl.semaphore_wait(barrier, 5)
+
+    @pl.when(end)
+    def _():
+        pl.semaphore_wait(barrier, 4)
+
 
     pending = []
     for n, peer in enumerate((sib, opp, diag)):
@@ -91,10 +102,19 @@
         pending.append(cp)
 
     send_x(0, tok_ref)
-    for i in (1, 2, 3):
-        cp = remote(tok_ref, xg.at[z, e], zs.at[i - 1], zr.at[i - 1], {"tensor": zi[i]})
-        cp.start()
-        pending.append(cp)
+    pending_inner = []
+
+    def send_z(n, src, shard, peer, only_inner):
+        cp = remote(src, xg.at[shard, e], zs.at[n], zr.at[shard], {"tensor": peer})
+        if only_inner:
+            pl.when(inner)(cp.start)
+            pending_inner.append(cp)
+        else:
+            cp.start()
+            pending.append(cp)
+
+    send_z(0, tok_ref, z, mate, False)
+    send_z(1, tok_ref, z, other, True)
     send_sib(0, 0, tok_ref, e)
 
     for k in range(CHUNKS):
@@ -106,7 +126,8 @@
 
     def arrived_z(i):
         here = xg.at[zi[i], e]
-        remote(here, here, zs.at[i - 1], zr.at[i - 1], {"tensor": zi[i]}).wait_recv()
+        remote(here, here, zs.at[0], zr.at[zi[i]], {"tensor": mate}).wait_recv()
+        send_z(i + 1, here, zi[i], other if i == 1 else mate, True)
         send_x(i, here)
         send_sib(0, i, here, e)
 
@@ -164,12 +185,14 @@
         def tile(n, carry):
             cols = pl.ds(pl.multiple_of(n * nt, nt), nt)
             g = jnp.dot(rows[j], wgu[slot, 0, :, cols], preferred_element_type=F32)
+            if i > 0:
+                g = g + acc[j, 0, :, cols]
+            if i < 3:
+                acc[j, 0, :, cols] = g
             u = jnp.dot(rows[j], wgu[slot, 1, :, cols], preferred_element_type=F32)
             if i > 0:
-                g = g + acc[j, 0, :, cols]
                 u = u + acc[j, 1, :, cols]
             if i < 3:
-                acc[j, 0, :, cols] = g
                 acc[j, 1, :, cols] = u
             else:
                 hidden[j, :, cols] = (g / (1.0 + jnp.exp(-g)) * u).astype(BF16)
@@ -209,15 +232,12 @@
         for cp in down_copies(k):
             cp.wait()
 
-        def tile(n, carry):
-            cols = pl.ds(pl.multiple_of(n * nt, nt), nt)
+        for n in range(0, width, 256):
+            cols = slice(n, n + 256)
             for j in range(2):
                 y = jnp.dot(hidden[j], wdn[slot, j, :, cols], preferred_element_type=F32).astype(BF16)
                 for b in range(4):
                     ybuf[b, pl.ds(j * half, half), cols] = y[b * half:(b + 1) * half]
-            return carry
-
-        lax.fori_loop(0, width // nt, tile, 0)
         if k + CHUNKS < 4:
             for cp in down_copies(k + CHUNKS):
                 cp.start()
@@ -244,24 +264,54 @@
         remote(here, here, xs2.at[k], xr2.at[k], {"expert": opp}).wait_recv()
         return keep[k, x].astype(F32) + core_in[k, x].astype(F32) + x_in[k].astype(F32)
 
-    def over_z(k):
-        i = order[k]
-        z_out[k] = summed(k).astype(BF16)
-        cp = remote(z_out.at[k], z_in.at[k], zs2.at[k], zr2.at[k], {"tensor": zi[i]})
-        cp.start()
-        pending.append(cp)
-
-    for k in range(4):
-        down(k)
-        over_x(k)
-        if k:
-            over_z(k - 1)
-    mine = summed(3)
+    def z_copy(k, slot, peer):
+        return remote(z_out.at[k], z_in.at[slot], zs2.at[k], zr2.at[slot], {"tensor": peer})
+
+    def z_arrived(slot):
+        here = z_in.at[slot]
+        remote(here, here, zs2.at[0], zr2.at[slot], {"tensor": mate}).wait_recv()
+        return z_in[slot].astype(F32)
+
+    def end_z(k):
+        @pl.when(end)
+        def _():
+            z_out[k] = summed(k).astype(BF16)
+            z_copy(k, (0, 1, 3)[k], mate).start()
+
+    def inner_z(k):
+        @pl.when(inner)
+        def _():
+            z_out[k] = (summed(k) + z_arrived(k)).astype(BF16)
+            z_copy(k, (2, 4, 3)[k], mate if k == 2 else other).start()
+
+    down(0)
+    over_x(0)
+    down(1)
+    over_x(1)
+    end_z(0)
+    down(2)
+    over_x(2)
+    inner_z(0)
+    end_z(1)
+    down(3)
+    over_x(3)
+    inner_z(1)
+    end_z(2)
+    inner_z(2)
+    mine = summed(3) + z_arrived(3)
+
+    @pl.when(end)
+    def _():
+        out_ref[...] = mine.astype(BF16)
+
+    @pl.when(inner)
+    def _():
+        out_ref[...] = (mine + z_arrived(4)).astype(BF16)
+
     for k in range(3):
-        here = z_in.at[k]
-        remote(here, here, zs2.at[k], zr2.at[k], {"tensor": zi[order[k]]}).wait_recv()
-        mine = mine + z_in[k].astype(F32)
-    out_ref[...] = mine.astype(BF16)
+        z_copy(k, 3, mate).wait_send()
+    for cp in pending_inner:
+        pl.when(inner)(cp.wait_send)
     for cp in pending:
         cp.wait_send()
 
@@ -300,10 +350,10 @@
             pltpu.VMEM((4, tok_rows, width), BF16),
             pltpu.VMEM((4, tok_rows, width), BF16),
             pltpu.VMEM((3, tok_rows, width), BF16),
-            pltpu.VMEM((3, tok_rows, width), BF16),
-            dma((3,)), dma((3,)), dma((3,)), dma((3,)), dma((4,)), dma((4,)),
+            pltpu.VMEM((5, tok_rows, width), BF16),
+            dma((3,)), dma((3,)), dma((5,)), dma((4,)), dma((4,)), dma((4,)),
             dma((2, 4)), dma((2, 4)), dma((PAIRS, 2)), dma((CHUNKS, 2)),
-            dma((4,)), dma((4,)), dma((4,)), dma((4,)), dma((3,)), dma((3,)),
+            dma((4,)), dma((4,)), dma((4,)), dma((4,)), dma((3,)), dma((5,)),
         ],
         compiler_params=pltpu.CompilerParams(
             collective_id=0, has_side_effects=True, vmem_limit_bytes=64 * 1024 * 1024
@@ -371,7 +421,7 @@
     def per_device(*args):
         tokens, gate_weight = args[0], args[3]
         fits = sizes == (4, 4) and gate_weight.shape[0] == 2 and tokens.shape[1] % 256 == 0
-        fits = fits and tokens.shape[0] == 128 and gate_weight.shape[2] % 256 == 0
+        fits = fits and tokens.shape[0] == 128 and gate_weight.shape[2] % 512 == 0
         return (fused if fits else on_device)(*args)
 
     return jax.shard_map(

time: 78.6 us -> 69.3 us (0.88)
  Pallas kernels: 74.7 us -> 65.4 us
    pallas_call x1, Pallas kernels: 74.7 us -> 65.4 us  [fused(): pl.pallas_call(layer_kernel, out_shape=jax.ShapeDtypeStruct((tok_rows, wi...]
where the time goes in v2:
time: 69.3 us; the launch traced here: 69.1 us
  Pallas kernels  65.4 us (94%)
  other arithmetic  2.02 us (3%)
  local copies, waits for them, and re-layouts  1.7 us (2%)
    pallas_call x1, Pallas kernels, fused(): pl.pallas_call(layer_kernel, out_shape=jax.ShapeDtypeStruct((tok_rows, wi...  65.4 us
    unnamed x1, local copies, waits for them, and re-layouts  1.62 us

profile of v2, /device:TPU:0, one launch (start us, length us, event | category | flops | bytes accessed | tf_op | source)
XLA Modules:
  0.0 69.1 jit_solution(681195052992462559)
XLA Ops:
  0.0 0.1 pad.2.clone
  0.1 0.7 convert_bitcast_fusion
  0.8 1.3 %maximum_maximum_fusion.meta_ref = f32[8,128]{1,0:T(8,128)} fusion(f32[2,128]{1,0:T(2,128)} %bitcast.3, f32[2,128]{1,0:T(2,128)S(1)} %convert_bitcast_fusion, f32[8]{0:T(128)S(1)} %pad.2.clone), kind=kLoop, calls=%fused_computation | loop fusion | flops 2048 | bytes 6176 | tf_op jit(solution)/shard_map/concatenate | solution.py:324
  2.1 65.4 %shard_map.64 = bf16[128,768]{1,0:T(8,128)(2,1)} custom-call(f32[8,128]{1,0:T(8,128)} %maximum_maximum_fusion.meta_ref, bf16[128,768]{1,0:T(8,128)(2,1)} %tok_ref.1, bf16[2,3072,2048]{2,1,0:T(8,128)(2,1)} %gate_hbm.1, bf16[2,3072,2048]{2,1,0:T(8,128)(2,1)} %up_hbm.1, bf16[2,2048,3072]{2,1,0:T(8,128)(2,1)} %down_hbm.1), custom_call_target="tpu_custom_call" | custom-call | flops 19327352832 | bytes 75497472 | tf_op jit(solution)/shard_map/pallas_call | solution.py:331
  67.5 1.6 %copy.8 = bf16[128,768]{1,0:T(8,128)(2,1)} copy(bf16[128,768]{1,0:T(8,128)(2,1)} %shard_map.64) | data formatting | bytes 393216
  (1 shorter events, 0.0 us)
